TPU v7x, 128 devices: a whole 4x4x4 slice. The times are simulated.
128 devices in a mesh: dp: 16 (over x, z), tensor: 8 (over y, core).
Axes of the slice: x: 4, y: 4, z: 4, core: 2. Of those that a mesh axis runs over, the one named last changes fastest.
Arguments:
- activations: bfloat16 [16384, 6144], P('dp', 'tensor'), may hold values from -6 to 6
- out_grads: bfloat16 [16384, 6144], P(('dp', 'tensor')), may hold values from -0.1875 to 0.1875
- feedback: bfloat16 [16, 6144, 6144], P('dp', 'tensor'), may hold values from -6 to 6
- right_basis: float32 [6144, 32], replicated, may hold values from -0.078125 to 0.078125
Outputs:
- new_feedback: bfloat16 [16, 6144, 6144], P('dp', 'tensor')
- new_right: float32 [6144, 32], replicated
All inputs are finite; a program needn't handle non-finite values.
Results may differ from a plain program's by a relative error of at most 0.013.
Values may be sent and summed in bfloat16 or wider, within the bound.
A program may use at most 128 MiB of HBM per device.

v0:
```python
import jax
import jax.numpy as jnp
from jax import lax
from jax.sharding import PartitionSpec as P


def body(activations, out_grads, feedback, right_basis):
    highest = lax.Precision.HIGHEST
    replicas = lax.axis_size("dp")
    contract = (((0,), (0,)), ((), ()))
    carried = feedback[0].astype(jnp.float32)
    merged = carried + lax.dot_general(
        activations,
        lax.all_gather(out_grads, "tensor", axis=0, tiled=True),
        contract,
        preferred_element_type=jnp.float32,
    )
    left_part = jnp.dot(merged, right_basis, precision=highest)
    left_rows = lax.psum(left_part.astype(jnp.bfloat16), "dp").astype(jnp.float32)
    local_gram = jnp.dot(left_rows.T, left_rows, precision=highest)
    gram_matrix = lax.psum(local_gram, "tensor")
    factor = jnp.linalg.cholesky(gram_matrix)
    left_basis = jax.scipy.linalg.solve_triangular(factor, left_rows.T, lower=True).T
    right_part = lax.dot_general(merged, left_basis, contract, precision=highest)
    new_right = lax.psum(right_part, ("dp", "tensor")) / replicas
    updated = merged - jnp.dot(left_basis, new_right.T, precision=highest)
    new_feedback = updated.astype(jnp.bfloat16)[None]
    return (new_feedback, new_right)


def solution(mesh):
    in_specs = (P("dp", "tensor"), P(("dp", "tensor"), None), P("dp", "tensor", None), P())
    out_specs = (P("dp", "tensor", None), P())
    return jax.shard_map(body, mesh=mesh, in_specs=in_specs, out_specs=out_specs, check_vma=False)
```

profile of v0, /device:TPU:1, one launch (start us, length us, event | category | flops | bytes accessed | tf_op | source)
XLA Modules:
  0.0 408.3 jit_solution(86268480515760465)
XLA Ops:
  7.2 0.0 copy-start
  7.2 0.0 all-gather.2.cloned.1.call-start
  7.2 0.7 all-gather.2.cloned.1.call-update
  7.9 0.0 copy-start.2
  7.9 0.0 all-reduce.2.cloned.1.call-start
  8.0 72.8 %all-gather.2.cloned.1.call-done = bf16[1024,6144]{1,0:T(8,128)(2,1)} async-done(((bf16[128,6144]{1,0:T(8,128)(2,1)}), bf16[1024,6144]{1,0:T(8,128)(2,1)}) %all-gather.2.cloned.1.call-update) | async-done | bytes 12582928 | tf_op jit(solution)/shard_map/all_gather | solution.py:14
  80.7 0.0 copy-done
  80.7 19.3 %convert_add_fusion = f32[768,6144]{1,0:T(8,128)} fusion(bf16[1024,768]{1,0:T(8,128)(2,1)S(1)} %copy-done, bf16[1024,6144]{1,0:T(8,128)(2,1)} %all-gather.2.cloned.1.call-done, bf16[1,768,6144]{2,1,0:T(8,128)(2,1)} %param.6), kind=kOutput, calls=%fused_computation | convolution fusion | flops 9673113600 | bytes 42467328 | tf_op jit(solution)/shard_map/dot_general | solution.py:12
  100.1 20.0 %convolution_convert_fusion = bf16[768,32]{0,1:T(8,128)(2,1)S(1)} fusion(f32[768,6144]{1,0:T(8,128)} %convert_add_fusion, f32[6144,32]{0,1:T(8,128)S(1)} %copy-done.2), kind=kOutput, calls=%fused_computation.3 | convolution fusion | flops 1811963904 | bytes 19709952 | tf_op jit(solution)/shard_map/dot_general | solution.py:18
  120.1 60.7 %psum.21 = bf16[768,32]{0,1:T(8,128)(2,1)S(1)} all-reduce(bf16[768,32]{0,1:T(8,128)(2,1)S(1)} %convolution_convert_fusion), channel_id=1, replica_groups=mesh['dp'=16,'tensor'=8] {'dp'}, use_global_device_ids=true, to_apply=%region_0.0 | all-reduce | flops 24576 | bytes 98304 | tf_op jit(solution)/shard_map/psum | solution.py:19
  180.8 0.1 fusion.5
  180.9 34.3 %psum.22 = f32[32,32]{0,1:T(8,128)S(1)} all-reduce(f32[32,32]{0,1:T(8,128)S(1)} %fusion.5), channel_id=1, replica_groups=mesh['dp'=16,'tensor'=8] {'tensor'}, use_global_device_ids=true, to_apply=%region_1.0 | all-reduce | flops 1024 | bytes 8192 | tf_op jit(solution)/shard_map/psum | solution.py:21
  215.2 0.1 copy.7
  215.3 2.9 cholesky.16
  218.3 0.6 compare_reduce_fusion
  218.9 0.7 fusion.1
  219.6 2.4 custom-call.7
  222.0 0.3 fusion.2
  222.3 15.2 %fusion.6 = f32[6144,32]{0,1:T(8,128)} fusion(f32[768,6144]{1,0:T(8,128)} %convert_add_fusion, f32[32,768]{1,0:T(8,128)S(1)} %fusion.2), kind=kOutput, calls=%fused_computation.16 | convolution fusion | flops 1811939328 | bytes 19759104 | tf_op jit(solution)/shard_map/dot_general | solution.py:24
  237.5 0.0 all-reduce.2.cloned.1.call-update
  237.5 142.7 %all-reduce.2.cloned.1.call-done = f32[6144,32]{0,1:T(8,128)} async-done(((f32[6144,32]{0,1:T(8,128)}), f32[6144,32]{0,1:T(8,128)}) %all-reduce.2.cloned.1.call-update) | async-done | bytes 786448 | tf_op jit(solution)/shard_map/psum | solution.py:25
  380.3 1.2 broadcast_multiply_fusion
  381.4 0.0 copy-start.1
  381.5 20.0 %fusion = bf16[1,768,6144]{2,1,0:T(8,128)(2,1)} fusion(f32[768,6144]{1,0:T(8,128)} %convert_add_fusion, f32[32,768]{1,0:T(8,128)S(1)} %fusion.2, f32[6144,32]{0,1:T(8,128)S(1)} %broadcast_multiply_fusion), kind=kOutput, calls=%fused_computation.2 | convolution fusion | flops 1821376512 | bytes 29196288 | tf_op jit(solution)/shard_map/dot_general | solution.py:26
  (4 shorter events, 0.0 us)
Async XLA Ops:
  7.2 73.6 %copy-start = (bf16[1024,768]{1,0:T(8,128)(2,1)S(1)}, bf16[1024,768]{1,0:T(8,128)(2,1)}, u32[]{:S(2)}) copy-start(bf16[1024,768]{1,0:T(8,128)(2,1)} %param.4) | copy-start | bytes 4718596
  7.2 73.5 %all-gather.2.cloned.1.call-start = ((), (), s32[]{:S(2)}) async-start(), calls=%async_computation | async-start | bytes 14155776 | tf_op jit(solution)/shard_map/all_gather | solution.py:14
  7.9 92.2 %copy-start.2 = (f32[6144,32]{0,1:T(8,128)S(1)}, f32[6144,32]{0,1:T(8,128)}, u32[]{:S(2)}) copy-start(f32[6144,32]{0,1:T(8,128)} %param.7) | copy-start | bytes 2359300
  7.9 372.3 %all-reduce.2.cloned.1.call-start = ((), (), s32[]{:S(2)}) async-start(), calls=%async_computation.1 | async-start | bytes 1572864 | tf_op jit(solution)/shard_map/psum | solution.py:25
  381.4 20.0 %copy-start.1 = (f32[6144,32]{0,1:T(8,128)}, f32[6144,32]{0,1:T(8,128)S(1)}, u32[]{:S(2)}) copy-start(f32[6144,32]{0,1:T(8,128)S(1)} %broadcast_multiply_fusion) | copy-start | bytes 2359300
Sparse Core Ops, SparseCore 0:
  9.7 70.9 all-gather.1
  237.7 142.5 all-reduce.1
where the time goes:
time: 409 us; the launch traced here: 408 us
  waiting for transfers between devices  216 us (53%)
  blocking collectives  95.1 us (23%)
  matrix products  74.9 us (18%)
  between operations  14.1 us (3%)
  other arithmetic  7.87 us (2%)
    psum x1, waiting for transfers between devices, body(): new_right = lax.psum(right_part, ('dp', 'tensor')) / replicas  143 us
    all_gather x1, waiting for transfers between devices, body(): lax.all_gather(out_grads, 'tensor', axis=0, tiled=True)  72.8 us
    psum x1, blocking collectives, body(): lax.psum(left_part.astype(jnp.bfloat16), 'dp').astype(jnp.float32)  60.7 us
    psum x1, blocking collectives, body(): gram_matrix = lax.psum(local_gram, 'tensor')  34.3 us
    dot_general x1, matrix products, body(): left_part = jnp.dot(merged, right_basis, precision=highest)  20 us
    dot_general x1, matrix products, body(): updated = merged - jnp.dot(left_basis, new_right.T, precision=highest)  20 us
    dot_general x1, matrix products, body(): lax.dot_general(activations, lax.all_gather(out_grads, 'tensor', axis=0,...  19.3 us
    dot_general x1, matrix products, body(): lax.dot_general(merged, left_basis, contract, precision=highest)  15.2 us
  transfers between devices with their start and end apart: 2, of which 2 were waited for; matrix products, arithmetic and copies ran while one was open for 0% of the time, Pallas kernels for 0%

commit v1 on v0

v1 whole, which is shorter than its diff:
```python
import functools

import jax
import jax.numpy as jnp
from jax import lax
from jax.experimental import pallas as pl
from jax.experimental.pallas import tpu as pltpu
from jax.sharding import PartitionSpec as P

MESH = pl.DeviceIdType.MESH
F32 = jnp.float32
BF16 = jnp.bfloat16
HIGHEST = lax.Precision.HIGHEST
RANK = 32
NY = 4
NT = 8
CHUNKS = 12
ROWS_FIRST = (((1,), (0,)), ((), ()))
ROWS_BOTH = (((1,), (1,)), ((), ()))


def dot(a, b, dims=ROWS_FIRST, precision=None):
    return lax.dot_general(a, b, dims, precision=precision, preferred_element_type=F32)


def split2(x):
    high = x.astype(BF16)
    low = (x - high.astype(F32)).astype(BF16)
    return high, low


def inverse_factor(gram):
    row = lax.broadcasted_iota(jnp.int32, (RANK, 128), 0)
    lane = lax.broadcasted_iota(jnp.int32, (RANK, 128), 1)
    work = jnp.where(lane < RANK, gram, jnp.where(lane == row + RANK, 1.0, 0.0))
    for k in range(RANK):
        column = jnp.broadcast_to(work[:, k : k + 1], (RANK, 128))
        pivot = column[k : k + 1, :]
        inv = lax.rsqrt(pivot)
        inv = inv * (1.5 - 0.5 * pivot * inv * inv)
        scaled = work[k : k + 1, :] * inv
        factor = jnp.where(row > k, column * inv, 0.0)
        work = jnp.where(row == k, scaled, work - factor * scaled)
    return work[:, RANK : 2 * RANK]


def chain_kernel(
    nx, nz,
    a_hbm, g_hbm, f_hbm, q_hbm,
    merged, p3, right,
    a_v, at_v, g_v, f_v, q_v, q2_v, gq_s, fq_v,
    la1, lb1, la2, lb2, left_v, left2_v,
    al_send, al_s, al2_v, linv_v,
    z_v, zsib, rs_s, y_s, zf,
    load_sem, dir_r, rel_r, sib_r, own_r, gq_r, l1_r, l2_r, al_r, zs_r, rs_r, y_r, ag_r, zf_r, send_sem,
):
    tok, d = g_hbm.shape
    feat = f_hbm.shape[0]
    half = d // 2
    piece_r, piece_c = RANK // nx, half // nz
    cw = d // CHUNKS
    dp, t = lax.axis_index("dp"), lax.axis_index("tensor")
    x, z = dp // nz, dp % nz
    y, c = t // 2, t % 2
    yp, ym, y2 = (y + 1) % NY, (y + 3) % NY, (y + 2) % NY
    sib = (dp, y * 2 + 1 - c)

    def at_y(yy):
        return (dp, yy * 2 + c)

    def rows(tt, first=0, count=None):
        return pl.ds(pl.multiple_of(tt * tok + first, 16), tok if count is None else count)

    def cols(j):
        return pl.ds(j * cw, cw)

    def remote(src, dst, send, recv, device):
        return pltpu.make_async_remote_copy(
            src_ref=src, dst_ref=dst, send_sem=send, recv_sem=recv, device_id=device, device_id_type=MESH
        )

    dp_peers = [
        (((x + i) % nx), ((z + k) % nz)) for i in range(nx) for k in range(nz) if i or k
    ]
    t_peers = [(t + k) % NT for k in range(1, NT)]

    g_load = pltpu.make_async_copy(g_hbm, g_v.at[rows(t), :], load_sem.at[0])
    q_load = pltpu.make_async_copy(q_hbm, q_v, load_sem.at[1])
    f_load = pltpu.make_async_copy(f_hbm, f_v, load_sem.at[2])
    a_load = pltpu.make_async_copy(a_hbm, a_v, load_sem.at[3])
    g_load.start()
    q_load.start()
    f_load.start()
    a_load.start()

    barrier = pltpu.get_barrier_semaphore()
    for tt in t_peers:
        pl.semaphore_signal(barrier, 1, device_id=(dp, tt), device_id_type=MESH)
    for xx, zz in dp_peers:
        pl.semaphore_signal(barrier, 1, device_id=(xx * nz + zz, t), device_id_type=MESH)
    q_load.wait()
    q_high, q_low = split2(q_v[...])
    q2_v[...] = jnp.concatenate([q_high, q_low], axis=0)
    g_load.wait()
    pl.semaphore_wait(barrier, len(t_peers) + len(dp_peers))

    def own_to_sib():
        return remote(g_v.at[rows(t), :], g_v.at[rows(t), :], send_sem.at[0], own_r, sib)

    def own_from_sib():
        block = g_v.at[rows(sib[1]), :]
        return remote(block, block, send_sem.at[0], own_r, sib)

    def send_dir(j):
        block = g_v.at[rows(t), cols(j)]
        remote(block, block, send_sem.at[1], dir_r.at[2 * j], at_y(yp)).start()
        remote(block, block, send_sem.at[2], dir_r.at[2 * j + 1], at_y(ym)).start()

    def fwd(tt, j, k):
        block = g_v.at[rows(tt), cols(j)]
        remote(block, block, send_sem.at[3 + k], sib_r.at[3 * j + k], sib).start()

    def take(tt, j, sem, first=0, count=None):
        block = g_v.at[rows(tt, first, count), cols(j)]
        remote(block, block, send_sem.at[0], sem, sib).wait_recv()

    def relay(j):
        take(ym * 2 + c, j, dir_r.at[2 * j])
        block = g_v.at[rows(ym * 2 + c, 0, tok // 2), cols(j)]
        remote(block, block, send_sem.at[6], rel_r.at[2 * j], at_y(yp)).start()
        take(yp * 2 + c, j, dir_r.at[2 * j + 1])
        block = g_v.at[rows(yp * 2 + c, tok // 2, tok // 2), cols(j)]
        remote(block, block, send_sem.at[7], rel_r.at[2 * j + 1], at_y(ym)).start()

    def opposite(j):
        take(y2 * 2 + c, j, rel_r.at[2 * j], 0, tok // 2)
        take(y2 * 2 + c, j, rel_r.at[2 * j + 1], tok // 2, tok // 2)
        fwd(y2 * 2 + c, j, 2)

    def pump(j):
        relay(j)
        if j + 2 < CHUNKS:
            send_dir(j + 2)
        fwd(ym * 2 + c, j, 0)
        fwd(yp * 2 + c, j, 1)
        if j >= 2:
            opposite(j - 2)

    def merge(j):
        if j == 0:
            own_from_sib().wait_recv()
        take(ym * 2 + 1 - c, j, sib_r.at[3 * j])
        take(yp * 2 + 1 - c, j, sib_r.at[3 * j + 1])
        take(y2 * 2 + 1 - c, j, sib_r.at[3 * j + 2])
        width = min(256, cw)

        def step(i, carry):
            at = pl.ds(pl.multiple_of(j * cw + i * width, 128), width)
            merged[:, at] = dot(at_v[...], g_v[:, at]) + f_v[:, at].astype(F32)
            return carry

        lax.fori_loop(0, cw // width, step, 0)

    own_to_sib().start()
    send_dir(0)

    gq2 = dot(q2_v[...], g_v[rows(t), :], ROWS_BOTH)
    gq_s[t] = gq2[:RANK] + gq2[RANK:]
    for tt in t_peers:
        remote(gq_s.at[t], gq_s.at[t], send_sem.at[8], gq_r.at[t], (dp, tt)).start()
    send_dir(1)

    f_load.wait()
    depth = d // 3
    for k in range(d // depth):
        at = pl.ds(k * depth, depth)
        part = dot(f_v[:, at], q2_v[:, at], ROWS_BOTH)
        if k == 0:
            fq_v[...] = part
        else:
            fq_v[...] += part
    a_load.wait()
    for k in range(NT):
        at_v[:, k * tok : (k + 1) * tok] = jnp.transpose(a_v[k * tok : (k + 1) * tok, :])
    pump(0)

    for tt in t_peers:
        remote(gq_s.at[tt], gq_s.at[tt], send_sem.at[8], gq_r.at[tt], sib).wait_recv()
    gq = jnp.concatenate([gq_s[k] for k in range(NT)], axis=1)
    part = dot(jnp.concatenate(split2(gq), axis=0), a_v[...])
    fq = fq_v[...]
    left_part = part[:RANK] + part[RANK:] + jnp.transpose(fq[:, :RANK] + fq[:, RANK:])

    hr = RANK // 2
    la1[x] = left_part[:hr].astype(BF16)
    lb1[z] = left_part[hr:].astype(BF16)

    def x_peers():
        return [((x + i) % nx) for i in range(1, nx)]

    def z_peers():
        return [((z + i) % nz) for i in range(1, nz)]

    def left_stage(slots_x, slots_z, sems, sem_at, start):
        for xx in x_peers():
            if start:
                remote(slots_x.at[x], slots_x.at[x], send_sem.at[sem_at], sems.at[x], (xx * nz + z, t)).start()
            else:
                remote(slots_x.at[xx], slots_x.at[xx], send_sem.at[sem_at], sems.at[xx], sib).wait_recv()
        for zz in z_peers():
            if start:
                remote(slots_z.at[z], slots_z.at[z], send_sem.at[sem_at + 1], sems.at[nx + z], (x * nz + zz, t)).start()
            else:
                remote(slots_z.at[zz], slots_z.at[zz], send_sem.at[sem_at + 1], sems.at[nx + zz], sib).wait_recv()

    def total(slots, n):
        out = slots[0].astype(F32)
        for k in range(1, n):
            out = out + slots[k].astype(F32)
        return out

    left_stage(la1, lb1, l1_r, 9, True)
    pump(1)
    left_stage(la1, lb1, l1_r, 9, False)
    la2[z] = total(la1, nx).astype(BF16)
    lb2[x] = total(lb1, nz).astype(BF16)
    left_stage(lb2, la2, l2_r, 11, True)
    pump(2)
    left_stage(lb2, la2, l2_r, 11, False)
    left_v[:hr] = total(la2, nz)
    left_v[hr:] = total(lb2, nx)
    left = left_v[...]
    left2_v[...] = jnp.concatenate(split2(left), axis=0)

    al = dot(left2_v[...], at_v[...])
    al = al[:RANK] + al[RANK:]
    gram = jnp.concatenate(
        [dot(left, left, ROWS_BOTH, HIGHEST), jnp.zeros((RANK, 128 - RANK), F32)], axis=1
    )
    for k in range(NT):
        al_send[k, :RANK] = al[:, k * tok : (k + 1) * tok]
        al_send[k, RANK:] = gram
    pump(3)
    for tt in t_peers:
        remote(al_send.at[tt], al_s.at[t], send_sem.at[13], al_r.at[t], (dp, tt)).start()
    al_s[t] = al_send[t]

    zw = min(512, d)

    def z_first(i, carry):
        at = pl.ds(pl.multiple_of(i * zw, 128), zw)
        r = dot(left2_v[...], f_v[:, at])
        z_v[:, at] = r[:RANK] + r[RANK:]
        return carry

    lax.fori_loop(0, d // zw, z_first, 0)
    pump(4)
    for tt in t_peers:
        remote(al_s.at[tt], al_s.at[tt], send_sem.at[13], al_r.at[tt], sib).wait_recv()
    al_sum = total(al_s, NT)
    al2_v[...] = jnp.concatenate(split2(al_sum[:RANK]), axis=0)
    linv_v[...] = jnp.concatenate([al_sum[RANK:], al_sum[RANK:]], axis=0)[:RANK]

    hw = min(512, half)

    def z_second(base):
        def step(i, carry):
            at = pl.ds(pl.multiple_of(base + i * hw, 128), hw)
            r = dot(al2_v[...], g_v[rows(t), at])
            z_v[:, at] += r[:RANK] + r[RANK:]
            return carry

        lax.fori_loop(0, half // hw, step, 0)

    mine, other = c * half, (1 - c) * half
    my_half = pl.ds(pl.multiple_of(mine, 128), half)
    sib_half = pl.ds(pl.multiple_of(other, 128), half)
    z_second(other)
    remote(z_v.at[:, sib_half], zsib, send_sem.at[14], zs_r, sib).start()
    z_second(mine)
    pump(5)
    remote(zsib, zsib, send_sem.at[14], zs_r, sib).wait_recv()
    z_v[:, my_half] += zsib[...]

    def piece(xx, zz):
        return (
            pl.ds(pl.multiple_of(xx * piece_r, 8), piece_r),
            pl.ds(pl.multiple_of(mine + zz * piece_c, 128), piece_c),
        )

    for xx, zz in dp_peers:
        remote(z_v.at[piece(xx, zz)], rs_s.at[dp], send_sem.at[15], rs_r.at[dp], (xx * nz + zz, t)).start()
    rs_s[dp] = z_v[piece(x, z)]
    linv = inverse_factor(linv_v[...])
    linv_v[:, :RANK] = linv
    left = left_v[...]
    p_high, p_low = split2(dot(linv, left, precision=HIGHEST))
    p_rows = jnp.concatenate([p_high, p_high, p_low, jnp.zeros((RANK, feat), BF16)], axis=0)
    p3[...] = jnp.transpose(p_rows.astype(F32)).astype(BF16)
    pump(6)
    merge(0)
    merge(1)
    for xx, zz in dp_peers:
        src = xx * nz + zz
        remote(rs_s.at[src], rs_s.at[src], send_sem.at[15], rs_r.at[src], sib).wait_recv()
    y_s[y] = total(rs_s, nx * nz)
    for yy in (yp, y2, ym):
        remote(y_s.at[y], y_s.at[y], send_sem.at[16], y_r.at[y], at_y(yy)).start()
    pump(7)
    merge(2)
    merge(3)
    for yy in (yp, y2, ym):
        remote(y_s.at[yy], y_s.at[yy], send_sem.at[16], y_r.at[yy], sib).wait_recv()
    zf[piece(x, z)] = total(y_s, NY)
    for xx, zz in dp_peers:
        remote(zf.at[piece(x, z)], zf.at[piece(x, z)], send_sem.at[17], ag_r.at[dp], (xx * nz + zz, t)).start()
    pump(8)
    merge(4)
    merge(5)
    pump(9)
    merge(6)
    merge(7)
    for xx, zz in dp_peers:
        src = xx * nz + zz
        remote(zf.at[piece(xx, zz)], zf.at[piece(xx, zz)], send_sem.at[17], ag_r.at[src], sib).wait_recv()
    remote(zf.at[:, my_half], zf.at[:, my_half], send_sem.at[18], zf_r, sib).start()
    pump(10)
    merge(8)
    remote(zf.at[:, sib_half], zf.at[:, sib_half], send_sem.at[18], zf_r, sib).wait_recv()
    linv = linv_v[:, :RANK]

    def finish(i, carry):
        at = pl.ds(pl.multiple_of(i * zw, 128), zw)
        right[:, at] = dot(linv, zf[:, at], precision=HIGHEST) * (1.0 / (nx * nz))
        return carry

    lax.fori_loop(0, d // zw, finish, 0)
    pump(11)
    merge(9)
    opposite(CHUNKS - 2)
    opposite(CHUNKS - 1)
    merge(10)
    merge(11)

    def sent(ref, sem):
        remote(ref, ref, send_sem.at[sem], own_r, sib).wait_send()

    own = g_v.at[rows(t), :]
    for k in range(6):
        sent(own, k)
    sent(g_v.at[rows(t, 0, tok // 2), :], 6)
    sent(g_v.at[rows(t, 0, tok // 2), :], 7)
    sent(gq_s.at[pl.ds(0, NT - 1)], 8)
    if nx > 1:
        sent(la1.at[pl.ds(0, nx - 1)], 9)
        sent(lb2.at[pl.ds(0, nx - 1)], 11)
    if nz > 1:
        sent(lb1.at[pl.ds(0, nz - 1)], 10)
        sent(la2.at[pl.ds(0, nz - 1)], 12)
    sent(al_s.at[pl.ds(0, NT - 1)], 13)
    sent(zsib, 14)
    sent(rs_s.at[pl.ds(0, nx * nz - 1)], 15)
    sent(y_s.at[pl.ds(0, NY - 1)], 16)
    sent(rs_s.at[pl.ds(0, nx * nz - 1)], 17)
    sent(zsib, 18)


def update_kernel(merged, p3, right, out, right_out, stage, r3_v, sems, right_sem):
    d = merged.shape[1]
    width = stage.shape[2]
    steps = d // width
    right_copy = pltpu.make_async_copy(right, right_out, right_sem)
    right_copy.start()

    def block(i):
        return pl.ds(pl.multiple_of(i * width, 128), width)

    def copy(i):
        return pltpu.make_async_copy(stage.at[i % 2], out.at[:, block(i)], sems.at[i % 2])

    for i in range(steps):
        r_high, r_low = split2(right[:, block(i)])
        r3_v[...] = jnp.concatenate([r_high, r_low, r_high, jnp.zeros((RANK, width), BF16)], axis=0)
        if i >= 2:
            copy(i - 2).wait()
        stage[i % 2] = (merged[:, block(i)] - dot(p3[...], r3_v[...])).astype(BF16)
        copy(i).start()
    copy(steps - 2).wait()
    copy(steps - 1).wait()
    right_copy.wait()


def body(nx, nz, activations, out_grads, feedback, right_basis):
    tokens, feat = activations.shape
    tok, d = out_grads.shape
    half = d // 2
    piece = (RANK // nx, half // nz)
    any_spec = pl.BlockSpec(memory_space=pl.ANY)
    vmem_spec = pl.BlockSpec(memory_space=pltpu.VMEM)
    dma = pltpu.SemaphoreType.DMA
    merged, p3, right = pl.pallas_call(
        functools.partial(chain_kernel, nx, nz),
        out_shape=(
            pltpu.VMEM((feat, d), F32),
            pltpu.VMEM((feat, 128), BF16),
            pltpu.VMEM((RANK, d), F32),
        ),
        in_specs=[any_spec] * 4,
        out_specs=(vmem_spec,) * 3,
        scratch_shapes=[
            pltpu.VMEM((tokens, feat), BF16),
            pltpu.VMEM((feat, tokens), BF16),
            pltpu.VMEM((tokens, d), BF16),
            pltpu.VMEM((feat, d), BF16),
            pltpu.VMEM((RANK, d), F32),
            pltpu.VMEM((2 * RANK, d), BF16),
            pltpu.VMEM((NT, RANK, tok), F32),
            pltpu.VMEM((feat, 2 * RANK), F32),
            pltpu.VMEM((nx, RANK // 2, feat), BF16),
            pltpu.VMEM((nz, RANK // 2, feat), BF16),
            pltpu.VMEM((nz, RANK // 2, feat), BF16),
            pltpu.VMEM((nx, RANK // 2, feat), BF16),
            pltpu.VMEM((RANK, feat), F32),
            pltpu.VMEM((2 * RANK, feat), BF16),
            pltpu.VMEM((NT, 2 * RANK, tok), F32),
            pltpu.VMEM((NT, 2 * RANK, tok), F32),
            pltpu.VMEM((2 * RANK, tok), BF16),
            pltpu.VMEM((RANK, 128), F32),
            pltpu.VMEM((RANK, d), F32),
            pltpu.VMEM((RANK, half), F32),
            pltpu.VMEM((nx * nz,) + piece, F32),
            pltpu.VMEM((NY,) + piece, F32),
            pltpu.VMEM((RANK, d), F32),
            dma((4,)),
            dma((2 * CHUNKS,)),
            dma((2 * CHUNKS,)),
            dma((3 * CHUNKS,)),
            dma,
            dma((NT,)),
            dma((nx + nz,)),
            dma((nx + nz,)),
            dma((NT,)),
            dma,
            dma((nx * nz,)),
            dma((NY,)),
            dma((nx * nz,)),
            dma,
            dma((19,)),
        ],
        compiler_params=pltpu.CompilerParams(
            collective_id=0, has_side_effects=True, vmem_limit_bytes=VMEM_LIMIT
        ),
        name="gather_and_factors",
    )(activations, out_grads, feedback[0], right_basis.T)
    width = min(512, d // 2)
    vmem = functools.partial(pltpu.with_memory_space_constraint, memory_space=pltpu.VMEM)
    new_feedback, new_right = pl.pallas_call(
        update_kernel,
        out_shape=(
            jax.ShapeDtypeStruct((feat, d), BF16),
            jax.ShapeDtypeStruct((RANK, d), F32),
        ),
        in_specs=[vmem_spec] * 3,
        out_specs=(any_spec, any_spec),
        scratch_shapes=[
            pltpu.VMEM((2, feat, width), BF16),
            pltpu.VMEM((128, width), BF16),
            dma((2,)),
            dma,
        ],
        compiler_params=pltpu.CompilerParams(vmem_limit_bytes=8 << 20),
        name="update",
    )(vmem(merged), vmem(p3), vmem(right))
    return new_feedback[None], new_right.T


VMEM_LIMIT = 40 << 20


def solution(mesh):
    nx = nz = 4
    in_specs = (P("dp", "tensor"), P(("dp", "tensor"), None), P("dp", "tensor", None), P())
    out_specs = (P("dp", "tensor", None), P())
    return jax.shard_map(
        functools.partial(body, nx, nz), mesh=mesh, in_specs=in_specs, out_specs=out_specs, check_vma=False
    )
```

time: 409 us -> 83.3 us (0.20)
  waiting for transfers between devices: 216 us -> 0 us
  blocking collectives: 95.1 us -> 0 us
  Pallas kernels: 0 us -> 82.4 us
  matrix products: 74.9 us -> 0 us
  between operations: 14.1 us -> 0.8 us
  other arithmetic: 7.87 us -> 0 us
    psum x1 -> x0, waiting for transfers between devices: 143 us -> none  [body(): new_right = lax.psum(right_part, ('dp', 'tensor')) / replicas]
    psum x2 -> x0, blocking collectives: 95.1 us -> none  [the longest x1 60.7 us: body(): lax.psum(left_part.astype(jnp.bfloat16), 'dp').astype(jnp.float32)]
    pallas_call x0 -> x2, Pallas kernels: none -> 82.4 us  [the longest x1 74.7 us: body(): pl.pallas_call(functools.partial(chain_kernel, nx, nz), out_shape=(pltpu....]
    dot_general x5 -> x0, matrix products: 74.6 us -> none  [the longest x1 20 us: body(): left_part = jnp.dot(merged, right_basis, precision=highest)]
    all_gather x1 -> x0, waiting for transfers between devices: 72.8 us -> none  [body(): lax.all_gather(out_grads, 'tensor', axis=0, tiled=True)]
    another operation x5 -> x0, other arithmetic: 6.68 us -> none  [the longest x3 3.59 us: body(): factor = jnp.linalg.cholesky(gram_matrix)]
  transfers between devices with their start and end apart: 2 -> 0, of which waited for: 2 -> 0; matrix products, arithmetic and copies ran while one was open for 0% -> 0% of each run, Pallas kernels for 0% -> 0%
where the time goes in v1:
time: 83.3 us; the launch traced here: 83.2 us
  Pallas kernels  82.4 us (99%)
    pallas_call x1, Pallas kernels, body(): pl.pallas_call(functools.partial(chain_kernel, nx, nz), out_shape=(pltpu....  74.7 us
    pallas_call x1, Pallas kernels, body(): pl.pallas_call(update_kernel, out_shape=(jax.ShapeDtypeStruct((feat, d),...  7.71 us

profile of v1, /device:TPU:1, one launch (start us, length us, event | category | flops | bytes accessed | tf_op | source)
XLA Modules:
  0.0 83.2 jit_solution(9673150698781644752)
XLA Ops:
  0.6 74.7 %gather_and_factors.1 = (f32[768,6144]{1,0:T(8,128)S(1)}, bf16[768,128]{1,0:T(8,128)(2,1)S(1)}, f32[32,6144]{1,0:T(8,128)S(1)}) custom-call(bf16[1024,768]{1,0:T(8,128)(2,1)} %a_hbm.1, bf16[128,6144]{1,0:T(8,128)(2,1)} %g_hbm.1, bf16[768,6144]{1,0:T(8,128)(2,1)} %bitcast.4, f32[32,6144]{1,0:T(8,128)} %bitcast.5), custom_call_target="tpu_custom_call" | custom-call | tf_op jit(solution)/shard_map/gather_and_factors/pallas_call | solution.py:401
  75.3 7.7 %update.1 = (bf16[768,6144]{1,0:T(8,128)(2,1)}, f32[32,6144]{1,0:T(8,128)}) custom-call(f32[768,6144]{1,0:T(8,128)S(1)} %get-tuple-element.7.merged, bf16[768,128]{1,0:T(8,128)(2,1)S(1)} %get-tuple-element.8.p3, f32[32,6144]{1,0:T(8,128)S(1)} %get-tuple-element.9.right), custom_call_target="tpu_custom_call" | custom-call | tf_op jit(solution)/shard_map/update/pallas_call | solution.py:457

commit v2 on v0

v2 whole, which is shorter than its diff:
```python
import functools

import jax
import jax.numpy as jnp
from jax import lax
from jax.experimental import pallas as pl
from jax.experimental.pallas import tpu as pltpu
from jax.sharding import PartitionSpec as P

MESH = pl.DeviceIdType.MESH
F32 = jnp.float32
BF16 = jnp.bfloat16
HIGHEST = lax.Precision.HIGHEST
RANK = 32
NY = 4
NT = 8
WIDTHS = (256,) + (512,) * 11 + (256,)
STARTS = tuple(sum(WIDTHS[:k]) for k in range(len(WIDTHS)))
CHUNKS = len(WIDTHS)
ROWS_FIRST = (((1,), (0,)), ((), ()))
ROWS_BOTH = (((1,), (1,)), ((), ()))


def dot(a, b, dims=ROWS_FIRST, precision=None):
    return lax.dot_general(a, b, dims, precision=precision, preferred_element_type=F32)


def split2(x):
    high = x.astype(BF16)
    low = (x - high.astype(F32)).astype(BF16)
    return high, low


def split3(x):
    high, low = split2(x)
    return high, low, (x - high.astype(F32) - low.astype(F32)).astype(BF16)


def inverse_factor(gram):
    row = lax.broadcasted_iota(jnp.int32, (RANK, 128), 0)
    lane = lax.broadcasted_iota(jnp.int32, (RANK, 128), 1)
    work = jnp.where(lane < RANK, gram, jnp.where(lane == row + RANK, 1.0, 0.0))
    for k in range(RANK):
        column = jnp.broadcast_to(work[:, k : k + 1], (RANK, 128))
        pivot = column[k : k + 1, :]
        inv = lax.rsqrt(pivot)
        inv = inv * (1.5 - 0.5 * pivot * inv * inv)
        scaled = work[k : k + 1, :] * inv
        factor = jnp.where(row > k, column * inv, 0.0)
        work = jnp.where(row == k, scaled, work - factor * scaled)
    return work[:, RANK : 2 * RANK]


def chain_kernel(
    nx, nz, plan,
    a_hbm, g_hbm, f_hbm, q_hbm,
    merged, p3, right,
    a_v, at_v, g_v, f_v, q_v, q2_v, gq_s, fq_v,
    la1, lb1, la2, lb2, left_v, left2_v,
    al_send, al_sib, al_s, al_fwd, al_in, al2_v, linv_v,
    z_v, zsib, rs_s, y_s, zf,
    load_sem, dir_r, rel_r, sib_r, own_r, gq_r, l1_r, l2_r, als_r, al_r, ali_r, zs_r, rs_r, y_r, ag_r, zf_r, send_sem, round_sem,
):
    tok, d = g_hbm.shape
    feat = f_hbm.shape[0]
    half = d // 2
    piece_r, piece_c = RANK // nx, half // nz
    zw = min(512, d)
    hw = min(512, half)
    hr = RANK // 2
    dp, t = lax.axis_index("dp"), lax.axis_index("tensor")
    x, z = dp // nz, dp % nz
    y, c = t // 2, t % 2
    yp, ym, y2 = (y + 1) % NY, (y + 3) % NY, (y + 2) % NY
    sib = (dp, y * 2 + 1 - c)
    mine, other = c * half, (1 - c) * half
    my_half = pl.ds(pl.multiple_of(mine, 128), half)
    sib_half = pl.ds(pl.multiple_of(other, 128), half)
    dp_peers = [(((x + i) % nx), ((z + k) % nz)) for i in range(nx) for k in range(nz) if i or k]
    x_peers = [((x + i) % nx) for i in range(1, nx)]
    z_peers = [((z + i) % nz) for i in range(1, nz)]
    outgoing = []

    def at_y(yy):
        return (dp, yy * 2 + c)

    def rows(tt, first=0, count=None):
        return pl.ds(pl.multiple_of(tt * tok + first, 16), tok if count is None else count)

    def cols(j):
        return pl.ds(STARTS[j], WIDTHS[j])

    def remote(src, dst, send, recv, device):
        return pltpu.make_async_remote_copy(
            src_ref=src, dst_ref=dst, send_sem=send, recv_sem=recv, device_id=device, device_id_type=MESH
        )

    def send(src, dst, sem, recv, device):
        remote(src, dst, send_sem.at[sem], recv, device).start()
        outgoing.append(sem)

    def receive(ref, recv):
        remote(ref, ref, send_sem.at[0], recv, sib).wait_recv()

    def piece(xx, zz):
        return (
            pl.ds(pl.multiple_of((xx + NY - y) % nx * piece_r, 8), piece_r),
            pl.ds(pl.multiple_of(mine + zz * piece_c, 128), piece_c),
        )

    def total(slots, n):
        out = slots[0].astype(F32)
        for k in range(1, n):
            out = out + slots[k].astype(F32)
        return out

    loads = [
        pltpu.make_async_copy(g_hbm, g_v.at[rows(t), :], load_sem.at[0]),
        pltpu.make_async_copy(q_hbm, q_v, load_sem.at[1]),
        pltpu.make_async_copy(f_hbm, f_v, load_sem.at[2]),
        pltpu.make_async_copy(a_hbm, a_v, load_sem.at[3]),
    ]

    near = [(dp, (y * 2 + c + 2) % NT), (dp, (y * 2 + c + 6) % NT)]
    near += [(((x + i) % nx) * nz + z, t) for i in (1, nx - 1)] + [(x * nz + (z + i) % nz, t) for i in (1, nz - 1)]

    def enter():
        loads[0].start()
        loads[1].start()
        barrier = pltpu.get_barrier_semaphore()
        for device in near + [sib]:
            pl.semaphore_signal(barrier, 1, device_id=device, device_id_type=MESH)
        loads[0].wait()
        loads[2].start()
        loads[3].start()
        loads[1].wait()
        q2_v[...] = jnp.concatenate(split2(q_v[...]), axis=0)
        pl.semaphore_wait(barrier, len(near) + 1)

    def tell(k):
        for device in near[2:] if k else near:
            pl.semaphore_signal(round_sem.at[k], 1, device_id=device, device_id_type=MESH)

    def hear(k):
        pl.semaphore_wait(round_sem.at[k], len(near[2:] if k else near))

    def wait_load(k):
        loads[k].wait()


    def own():
        send(g_v.at[rows(t), :], g_v.at[rows(t), :], 0, own_r, sib)

    def direct(j):
        block = g_v.at[rows(t), cols(j)]
        send(block, block, 1, dir_r.at[2 * j], at_y(yp))
        send(block, block, 2, dir_r.at[2 * j + 1], at_y(ym))

    def to_sib(tt, j, k):
        block = g_v.at[rows(tt), cols(j)]
        send(block, block, 3 + k, sib_r.at[3 * j + k], sib)

    def relay(j):
        receive(g_v.at[rows(ym * 2 + c), cols(j)], dir_r.at[2 * j])
        block = g_v.at[rows(ym * 2 + c, 0, tok // 2), cols(j)]
        send(block, block, 6, rel_r.at[2 * j], at_y(yp))
        receive(g_v.at[rows(yp * 2 + c), cols(j)], dir_r.at[2 * j + 1])
        block = g_v.at[rows(yp * 2 + c, tok // 2, tok // 2), cols(j)]
        send(block, block, 7, rel_r.at[2 * j + 1], at_y(ym))

    def cross(j):
        to_sib(ym * 2 + c, j, 0)
        to_sib(yp * 2 + c, j, 1)

    def opposite(j):
        receive(g_v.at[rows(y2 * 2 + c, 0, tok // 2), cols(j)], rel_r.at[2 * j])
        receive(g_v.at[rows(y2 * 2 + c, tok // 2, tok // 2), cols(j)], rel_r.at[2 * j + 1])
        to_sib(y2 * 2 + c, j, 2)

    def pump(j):
        relay(j)
        if j + 3 < CHUNKS:
            direct(j + 3)
        cross(j)
        if j >= 2:
            opposite(j - 2)

    def absorb(j):
        if j == 0:
            receive(g_v.at[rows(sib[1]), :], own_r)
        for k, yy in enumerate((ym, yp, y2)):
            receive(g_v.at[rows(yy * 2 + 1 - c), cols(j)], sib_r.at[3 * j + k])

    def merge(j):
        absorb(j)
        width = min(256, WIDTHS[j])

        def step(i, carry):
            at = pl.ds(pl.multiple_of(STARTS[j] + i * width, 128), width)
            merged[:, at] = dot(at_v[...], g_v[:, at]) + f_v[:, at].astype(F32)
            return carry

        lax.fori_loop(0, WIDTHS[j] // width, step, 0)


    y_peers = (yp, y2, ym)

    def project():
        gq2 = dot(q2_v[...], g_v[rows(t), :], ROWS_BOTH)
        gq_s[c, y] = gq2[:RANK] + gq2[RANK:]

    def project_send():
        for yy in y_peers:
            send(gq_s.at[c, y], gq_s.at[c, y], 8, gq_r.at[y], at_y(yy))
        send(gq_s.at[c, y], gq_s.at[c, y], 19, gq_r.at[NY + y], sib)

    def project_cross():
        for yy in y_peers:
            receive(gq_s.at[c, yy], gq_r.at[yy])
            send(gq_s.at[c, yy], gq_s.at[c, yy], 19, gq_r.at[NY + yy], sib)

    def carried():
        wait_load(2)
        depth = d // 3
        for k in range(d // depth):
            at = pl.ds(k * depth, depth)
            part = dot(f_v[:, at], q2_v[:, at], ROWS_BOTH)
            if k == 0:
                fq_v[...] = part
            else:
                fq_v[...] += part

    def flip():
        wait_load(3)
        for k in range(NT):
            at_v[:, k * tok : (k + 1) * tok] = jnp.transpose(a_v[k * tok : (k + 1) * tok, :])

    def left_start():
        for yy in range(NY):
            receive(gq_s.at[1 - c, yy], gq_r.at[NY + yy])
        gq = jnp.concatenate([gq_s[k % 2, k // 2] for k in range(NT)], axis=1)
        part = dot(jnp.concatenate(split2(gq), axis=0), a_v[...])
        fq = fq_v[...]
        left_part = part[:RANK] + part[RANK:] + jnp.transpose(fq[:, :RANK] + fq[:, RANK:])
        la1[x] = left_part[:hr].astype(BF16)
        lb1[z] = left_part[hr:].astype(BF16)
        left_send(la1, lb1, l1_r, 9)

    def left_send(slots_x, slots_z, sems, at):
        for xx in x_peers:
            send(slots_x.at[x], slots_x.at[x], at, sems.at[x], (xx * nz + z, t))
        for zz in z_peers:
            send(slots_z.at[z], slots_z.at[z], at + 1, sems.at[nx + z], (x * nz + zz, t))

    def left_receive(slots_x, slots_z, sems):
        for xx in x_peers:
            receive(slots_x.at[xx], sems.at[xx])
        for zz in z_peers:
            receive(slots_z.at[zz], sems.at[nx + zz])

    def left_second():
        left_receive(la1, lb1, l1_r)
        la2[z] = total(la1, nx).astype(BF16)
        lb2[x] = total(lb1, nz).astype(BF16)
        left_send(lb2, la2, l2_r, 11)

    def left_end():
        left_receive(lb2, la2, l2_r)
        left_v[:hr] = total(la2, nz)
        left_v[hr:] = total(lb2, nx)
        left2_v[...] = jnp.concatenate(split2(left_v[...]), axis=0)

    def mapped():
        left = left_v[...]
        al = dot(left2_v[...], at_v[...])
        al = al[:RANK] + al[RANK:]
        gram = dot(left, left, ROWS_BOTH, HIGHEST)
        gram = jnp.concatenate([gram[8 * k : 8 * k + 8] for k in range(RANK // 8)], axis=1)
        for k in range(NT):
            al_send[k % 2, k // 2, :RANK] = al[:, k * tok : (k + 1) * tok]
            al_send[k % 2, k // 2, RANK:] = gram
        send(al_send.at[1 - c], al_sib, 20, als_r, sib)

    def mapped_send():
        receive(al_sib, als_r)
        al_send[c] += al_sib[...]
        for yy in y_peers:
            send(al_send.at[c, yy], al_s.at[y], 13, al_r.at[y], (((x + 1) % nx) * nz + z, yy * 2 + c))

    def mapped_relay():
        for yy in y_peers:
            receive(al_s.at[yy], al_r.at[yy])
        al_s[y] = al_send[c, y]
        fwd = al_s[yp, :RANK] + al_s[y2, :RANK] + al_s[ym, :RANK]
        al_fwd[...] = fwd
        send(al_fwd, al_in, 21, ali_r, (((x + nx - 1) % nx) * nz + z, t))
        gram = total(al_s, NY)[RANK:]
        gram = jnp.concatenate([gram[:, RANK * k : RANK * (k + 1)] for k in range(RANK // 8)], axis=0)
        linv_v[...] = jnp.concatenate([gram, jnp.zeros((RANK, 128 - RANK), F32)], axis=1)

    def z_first():
        def step(i, carry):
            at = pl.ds(pl.multiple_of(i * zw, 128), zw)
            r = dot(left2_v[...], f_v[:, at])
            z_v[:, at] = r[:RANK] + r[RANK:]
            return carry

        lax.fori_loop(0, d // zw, step, 0)

    def mapped_end():
        receive(al_in, ali_r)
        al2_v[...] = jnp.concatenate(split2(al_send[c, y, :RANK] + al_in[...]), axis=0)

    def z_second(base):
        def step(i, carry):
            at = pl.ds(pl.multiple_of(base + i * hw, 128), hw)
            r = dot(al2_v[...], g_v[rows(t), at])
            z_v[:, at] += r[:RANK] + r[RANK:]
            return carry

        lax.fori_loop(0, half // hw, step, 0)

    def z_send():
        z_second(other)
        send(z_v.at[:, sib_half], zsib, 14, zs_r, sib)
        z_second(mine)

    def z_scatter():
        receive(zsib, zs_r)
        z_v[:, my_half] += zsib[...]
        for xx, zz in dp_peers:
            send(z_v.at[piece(xx, zz)], rs_s.at[dp], 15, rs_r.at[dp], (xx * nz + zz, t))
        rs_s[dp] = z_v[piece(x, z)]

    def factor():
        linv = inverse_factor(linv_v[...])
        linv_v[:, :RANK] = linv
        p_high, p_low = split2(dot(linv, left_v[...], precision=HIGHEST))
        p_rows = jnp.concatenate([p_high, p_high, p_low, jnp.zeros((RANK, feat), BF16)], axis=0)
        p3[...] = jnp.transpose(p_rows.astype(F32)).astype(BF16)

    def z_over_y():
        for xx, zz in dp_peers:
            receive(rs_s.at[xx * nz + zz], rs_r.at[xx * nz + zz])
        y_s[y] = total(rs_s, nx * nz)
        for yy in (yp, y2, ym):
            send(y_s.at[y], y_s.at[y], 16, y_r.at[y], (((x + NY - y + yy) % nx) * nz + z, yy * 2 + c))

    def z_back():
        for yy in (yp, y2, ym):
            receive(y_s.at[yy], y_r.at[yy])
        zf[piece(x, z)] = total(y_s, NY)
        for xx, zz in dp_peers:
            send(zf.at[piece(x, z)], zf.at[piece(x, z)], 17, ag_r.at[dp], (xx * nz + zz, t))

    def z_cross():
        for xx, zz in dp_peers:
            receive(zf.at[piece(xx, zz)], ag_r.at[xx * nz + zz])
        send(zf.at[:, my_half], zf.at[:, my_half], 18, zf_r, sib)

    def z_end():
        receive(zf.at[:, sib_half], zf_r)

    def finish():
        l1, l2, l3 = split3(linv_v[:, :RANK])
        lhs = jnp.concatenate([l1, l1, l2, l1, l2, l3], axis=1)

        def step(i, carry):
            at = pl.ds(pl.multiple_of(i * zw, 128), zw)
            z1, z2, z3 = split3(zf[:, at])
            rhs = jnp.concatenate([z1, z2, z1, z3, z2, z1], axis=0)
            right[:, at] = dot(lhs, rhs) * (1.0 / (nx * nz))
            return carry

        lax.fori_loop(0, d // zw, step, 0)

    def leave():
        gather = [g_v.at[rows(t), :]] * 6 + [g_v.at[rows(t, 0, tok // 2), :]] * 2
        pieces = gather + [gq_s.at[0, pl.ds(0, NY - 1)]]
        for slots in (la1, lb1, lb2, la2):
            pieces.append(slots.at[pl.ds(0, slots.shape[0] - 1)])
        pieces += [al_s.at[pl.ds(0, NY - 1)], zsib, rs_s.at[pl.ds(0, nx * nz - 1)]]
        pieces += [y_s.at[pl.ds(0, NY - 1)], rs_s.at[pl.ds(0, nx * nz - 1)], zsib]
        pieces += [gq_s.at[0], al_sib, al_in]
        for sem, ref in enumerate(pieces):
            if sem in outgoing:
                remote(ref, ref, send_sem.at[sem], own_r, sib).wait_send()

    steps = dict(tell=tell, hear=hear, project_send=project_send, project_cross=project_cross,
        enter=enter, wait_load=wait_load, absorb=absorb, own=own, direct=direct, relay=relay, cross=cross, opposite=opposite, pump=pump, merge=merge,
        project=project, carried=carried, flip=flip, left_start=left_start, left_second=left_second,
        left_end=left_end, mapped=mapped, mapped_send=mapped_send, mapped_relay=mapped_relay, z_first=z_first, mapped_end=mapped_end,
        z_send=z_send, z_scatter=z_scatter, factor=factor, z_over_y=z_over_y, z_back=z_back, z_cross=z_cross,
        z_end=z_end, finish=finish, leave=leave,
    )
    for name, *args in plan:
        steps[name](*args)


def chain_plan():
    return [
        ("enter",), ("tell", 0), ("direct", 0), ("project",), ("hear", 0), ("project_send",), ("direct", 1),
        ("direct", 2), ("tell", 1), ("carried",), ("project_cross",), ("flip",), ("left_start",), ("own",),
        ("pump", 0), ("pump", 1), ("hear", 1), ("tell", 2), ("left_second",), ("pump", 2), ("left_end",),
        ("mapped",), ("mapped_send",), ("z_first",), ("pump", 3), ("mapped_relay",), ("pump", 4), ("hear", 2),
        ("mapped_end",), ("z_send",), ("pump", 5), ("z_scatter",), ("factor",), ("pump", 6), ("merge", 0),
        ("merge", 1), ("merge", 2), ("pump", 7), ("z_over_y",), ("merge", 3), ("merge", 4), ("merge", 5),
        ("pump", 8), ("z_back",), ("pump", 9), ("merge", 6), ("merge", 7), ("pump", 10), ("z_cross",),
        ("merge", 8), ("z_end",), ("pump", 11), ("finish",), ("merge", 9), ("pump", 12), ("merge", 10),
        ("opposite", 11), ("merge", 11), ("opposite", 12), ("merge", 12), ("leave",),
    ]


def update_kernel(merged, p3, right, out, right_out, stage, r3_v, sems, right_sem):
    d = merged.shape[1]
    width = stage.shape[2]
    steps = d // width
    right_copy = pltpu.make_async_copy(right, right_out, right_sem)
    right_copy.start()

    def block(i):
        return pl.ds(pl.multiple_of(i * width, 128), width)

    def copy(i):
        return pltpu.make_async_copy(stage.at[i], out.at[:, block(i)], sems.at[i])

    for i in range(steps):
        r_high, r_low = split2(right[:, block(i)])
        r3_v[...] = jnp.concatenate([r_high, r_low, r_high, jnp.zeros((RANK, width), BF16)], axis=0)
        stage[i] = (merged[:, block(i)] - dot(p3[...], r3_v[...])).astype(BF16)
        copy(i).start()
    for i in range(steps):
        copy(i).wait()
    right_copy.wait()


def body(nx, nz, activations, out_grads, feedback, right_basis):
    tokens, feat = activations.shape
    tok, d = out_grads.shape
    half = d // 2
    piece = (RANK // nx, half // nz)
    any_spec = pl.BlockSpec(memory_space=pl.ANY)
    vmem_spec = pl.BlockSpec(memory_space=pltpu.VMEM)
    dma = pltpu.SemaphoreType.DMA
    merged, p3, right = pl.pallas_call(
        functools.partial(chain_kernel, nx, nz, chain_plan()),
        out_shape=(
            pltpu.VMEM((feat, d), F32),
            pltpu.VMEM((feat, 128), BF16),
            pltpu.VMEM((RANK, d), F32),
        ),
        in_specs=[any_spec] * 4,
        out_specs=(vmem_spec,) * 3,
        scratch_shapes=[
            pltpu.VMEM((tokens, feat), BF16),
            pltpu.VMEM((feat, tokens), BF16),
            pltpu.VMEM((tokens, d), BF16),
            pltpu.VMEM((feat, d), BF16),
            pltpu.VMEM((RANK, d), F32),
            pltpu.VMEM((2 * RANK, d), BF16),
            pltpu.VMEM((2, NY, RANK, tok), F32),
            pltpu.VMEM((feat, 2 * RANK), F32),
            pltpu.VMEM((nx, RANK // 2, feat), BF16),
            pltpu.VMEM((nz, RANK // 2, feat), BF16),
            pltpu.VMEM((nz, RANK // 2, feat), BF16),
            pltpu.VMEM((nx, RANK // 2, feat), BF16),
            pltpu.VMEM((RANK, feat), F32),
            pltpu.VMEM((2 * RANK, feat), BF16),
            pltpu.VMEM((2, NY, RANK + 8, tok), F32),
            pltpu.VMEM((NY, RANK + 8, tok), F32),
            pltpu.VMEM((NY, RANK + 8, tok), F32),
            pltpu.VMEM((RANK, tok), F32),
            pltpu.VMEM((RANK, tok), F32),
            pltpu.VMEM((2 * RANK, tok), BF16),
            pltpu.VMEM((RANK, 128), F32),
            pltpu.VMEM((RANK, d), F32),
            pltpu.VMEM((RANK, half), F32),
            pltpu.VMEM((nx * nz,) + piece, F32),
            pltpu.VMEM((NY,) + piece, F32),
            pltpu.VMEM((RANK, d), F32),
            dma((4,)),
            dma((2 * CHUNKS,)),
            dma((2 * CHUNKS,)),
            dma((3 * CHUNKS,)),
            dma,
            dma((NT,)),
            dma((nx + nz,)),
            dma((nx + nz,)),
            dma,
            dma((NY,)),
            dma,
            dma,
            dma((nx * nz,)),
            dma((NY,)),
            dma((nx * nz,)),
            dma,
            dma((22,)),
            pltpu.SemaphoreType.REGULAR((3,)),
        ],
        compiler_params=pltpu.CompilerParams(
            collective_id=0, has_side_effects=True, vmem_limit_bytes=VMEM_LIMIT
        ),
        name="gather_and_factors",
    )(activations, out_grads, feedback[0], right_basis.T)
    width = min(512, d // 2)
    vmem = functools.partial(pltpu.with_memory_space_constraint, memory_space=pltpu.VMEM)
    new_feedback, new_right = pl.pallas_call(
        update_kernel,
        out_shape=(
            jax.ShapeDtypeStruct((feat, d), BF16),
            jax.ShapeDtypeStruct((RANK, d), F32),
        ),
        in_specs=[vmem_spec] * 3,
        out_specs=(any_spec, any_spec),
        scratch_shapes=[
            pltpu.VMEM((d // width, feat, width), BF16),
            pltpu.VMEM((128, width), BF16),
            dma((d // width,)),
            dma,
        ],
        compiler_params=pltpu.CompilerParams(vmem_limit_bytes=16 << 20),
        name="update",
    )(vmem(merged), vmem(p3), vmem(right))
    return new_feedback[None], new_right.T


VMEM_LIMIT = 40 << 20


def solution(mesh):
    nx = nz = 4
    in_specs = (P("dp", "tensor"), P(("dp", "tensor"), None), P("dp", "tensor", None), P())
    out_specs = (P("dp", "tensor", None), P())
    return jax.shard_map(
        functools.partial(body, nx, nz), mesh=mesh, in_specs=in_specs, out_specs=out_specs, check_vma=False
    )
```

time: 409 us -> 74.9 us (0.18)
  waiting for transfers between devices: 216 us -> 0 us
  blocking collectives: 95.1 us -> 0 us
  matrix products: 74.9 us -> 0 us
  Pallas kernels: 0 us -> 73.9 us
  between operations: 14.1 us -> 0.8 us
  other arithmetic: 7.87 us -> 0 us
    psum x1 -> x0, waiting for transfers between devices: 143 us -> none  [body(): new_right = lax.psum(right_part, ('dp', 'tensor')) / replicas]
    psum x2 -> x0, blocking collectives: 95.1 us -> none  [the longest x1 60.7 us: body(): lax.psum(left_part.astype(jnp.bfloat16), 'dp').astype(jnp.float32)]
    dot_general x5 -> x0, matrix products: 74.6 us -> none  [the longest x1 20 us: body(): left_part = jnp.dot(merged, right_basis, precision=highest)]
    pallas_call x0 -> x2, Pallas kernels: none -> 73.9 us  [the longest x1 69.6 us: body(): pl.pallas_call(functools.partial(chain_kernel, nx, nz, chain_plan()), out...]
    all_gather x1 -> x0, waiting for transfers between devices: 72.8 us -> none  [body(): lax.all_gather(out_grads, 'tensor', axis=0, tiled=True)]
    another operation x5 -> x0, other arithmetic: 6.68 us -> none  [the longest x3 3.59 us: body(): factor = jnp.linalg.cholesky(gram_matrix)]
  transfers between devices with their start and end apart: 2 -> 0, of which waited for: 2 -> 0; matrix products, arithmetic and copies ran while one was open for 0% -> 0% of each run, Pallas kernels for 0% -> 0%
where the time goes in v2:
time: 74.9 us; the launch traced here: 74.7 us
  Pallas kernels  73.9 us (99%)
  between operations  0.8 us (1%)
    pallas_call x1, Pallas kernels, body(): pl.pallas_call(functools.partial(chain_kernel, nx, nz, chain_plan()), out...  69.6 us
    pallas_call x1, Pallas kernels, body(): pl.pallas_call(update_kernel, out_shape=(jax.ShapeDtypeStruct((feat, d),...  4.32 us

profile of v2, /device:TPU:1, one launch (start us, length us, event | category | flops | bytes accessed | tf_op | source)
XLA Modules:
  0.0 74.7 jit_solution(7697794906430238092)
XLA Ops:
  0.6 69.6 %gather_and_factors.1 = (f32[768,6144]{1,0:T(8,128)S(1)}, bf16[768,128]{1,0:T(8,128)(2,1)S(1)}, f32[32,6144]{1,0:T(8,128)S(1)}) custom-call(bf16[1024,768]{1,0:T(8,128)(2,1)} %a_hbm.1, bf16[128,6144]{1,0:T(8,128)(2,1)} %g_hbm.1, bf16[768,6144]{1,0:T(8,128)(2,1)} %bitcast.4, f32[32,6144]{1,0:T(8,128)} %bitcast.5), custom_call_target="tpu_custom_call" | custom-call | tf_op jit(solution)/shard_map/gather_and_factors/pallas_call | solution.py:445
  70.3 4.3 %update.1 = (bf16[768,6144]{1,0:T(8,128)(2,1)}, f32[32,6144]{1,0:T(8,128)}) custom-call(f32[768,6144]{1,0:T(8,128)S(1)} %get-tuple-element.7.merged, bf16[768,128]{1,0:T(8,128)(2,1)S(1)} %get-tuple-element.8.p3, f32[32,6144]{1,0:T(8,128)S(1)} %get-tuple-element.9.right), custom_call_target="tpu_custom_call" | custom-call | tf_op jit(solution)/shard_map/update/pallas_call | solution.py:507

commit v3 on v2

--- a/solution.py
+++ b/solution.py
@@ -12,6 +12,7 @@
 BF16 = jnp.bfloat16
 HIGHEST = lax.Precision.HIGHEST
 RANK = 32
+AHEAD = 5
 NY = 4
 NT = 8
 WIDTHS = (256,) + (512,) * 11 + (256,)
@@ -59,7 +60,7 @@
     la1, lb1, la2, lb2, left_v, left2_v,
     al_send, al_sib, al_s, al_fwd, al_in, al2_v, linv_v,
     z_v, zsib, rs_s, y_s, zf,
-    load_sem, dir_r, rel_r, sib_r, own_r, gq_r, l1_r, l2_r, als_r, al_r, ali_r, zs_r, rs_r, y_r, ag_r, zf_r, send_sem, round_sem,
+    load_sem, dir_r, rel_r, sib_r, own_r, gq_r, l1_r, l2_r, als_r, al_r, ali_r, zs_r, rs_r, y_r, ag_r, zf_r, send_sem, round_sem, ring_sem,
 ):
     tok, d = g_hbm.shape
     feat = f_hbm.shape[0]
@@ -121,28 +122,48 @@
         pltpu.make_async_copy(a_hbm, a_v, load_sem.at[3]),
     ]
 
-    near = [(dp, (y * 2 + c + 2) % NT), (dp, (y * 2 + c + 6) % NT)]
-    near += [(((x + i) % nx) * nz + z, t) for i in (1, nx - 1)] + [(x * nz + (z + i) % nz, t) for i in (1, nz - 1)]
+    before = [(x > 0, (dp - nz, t)), (z > 0, (dp - 1, t))]
+    after = [(x < nx - 1, (dp + nz, t)), (z < nz - 1, (dp + 1, t))]
+    ring = [at_y(yp), at_y(ym)]
+
+    def signal(sem, devices):
+        for there, device in devices:
+
+            @pl.when(there)
+            def _():
+                pl.semaphore_signal(sem, 1, device_id=device, device_id_type=MESH)
+
+    def count(devices):
+        return sum(there.astype(jnp.int32) for there, _ in devices)
 
     def enter():
         loads[0].start()
         loads[1].start()
         barrier = pltpu.get_barrier_semaphore()
-        for device in near + [sib]:
+        for device in ring + [sib]:
             pl.semaphore_signal(barrier, 1, device_id=device, device_id_type=MESH)
+        signal(barrier, after)
         loads[0].wait()
         loads[2].start()
         loads[3].start()
         loads[1].wait()
         q2_v[...] = jnp.concatenate(split2(q_v[...]), axis=0)
-        pl.semaphore_wait(barrier, len(near) + 1)
+        pl.semaphore_wait(barrier, 3 + count(before))
+        for device in ring:
+            pl.semaphore_signal(ring_sem, 1, device_id=device, device_id_type=MESH)
+
+    def hear_ring():
+        pl.semaphore_wait(ring_sem, 2)
 
     def tell(k):
-        for device in near[2:] if k else near:
-            pl.semaphore_signal(round_sem.at[k], 1, device_id=device, device_id_type=MESH)
+        signal(round_sem.at[k], before + after if k else before)
 
     def hear(k):
-        pl.semaphore_wait(round_sem.at[k], len(near[2:] if k else near))
+        told = count(before + after if k else after)
+
+        @pl.when(told > 0)
+        def _():
+            pl.semaphore_wait(round_sem.at[k], told)
 
     def wait_load(k):
         loads[k].wait()
@@ -177,27 +198,39 @@
         receive(g_v.at[rows(y2 * 2 + c, tok // 2, tok // 2), cols(j)], rel_r.at[2 * j + 1])
         to_sib(y2 * 2 + c, j, 2)
 
-    def pump(j):
+    def pump(j, ahead=True):
         relay(j)
-        if j + 3 < CHUNKS:
-            direct(j + 3)
+        if ahead and j + AHEAD < CHUNKS:
+            direct(j + AHEAD)
         cross(j)
-        if j >= 2:
-            opposite(j - 2)
-
-    def absorb(j):
-        if j == 0:
+
+    def absorb(j, part=None):
+        if j == 0 and part != 1:
             receive(g_v.at[rows(sib[1]), :], own_r)
         for k, yy in enumerate((ym, yp, y2)):
-            receive(g_v.at[rows(yy * 2 + 1 - c), cols(j)], sib_r.at[3 * j + k])
-
-    def merge(j):
-        absorb(j)
+            if part is None or (part == 1) == (k == 2):
+                receive(g_v.at[rows(yy * 2 + 1 - c), cols(j)], sib_r.at[3 * j + k])
+
+    def merge(j, part=None):
+        absorb(j, part)
         width = min(256, WIDTHS[j])
+
+        def chips(at, *ys):
+            out = None
+            for yy in ys:
+                pair = pl.ds(pl.multiple_of(yy * 2 * tok, 2 * tok), 2 * tok)
+                term = dot(at_v[:, pair], g_v[pair, at])
+                out = term if out is None else out + term
+            return out
 
         def step(i, carry):
             at = pl.ds(pl.multiple_of(STARTS[j] + i * width, 128), width)
-            merged[:, at] = dot(at_v[...], g_v[:, at]) + f_v[:, at].astype(F32)
+            if part is None:
+                merged[:, at] = dot(at_v[...], g_v[:, at]) + f_v[:, at].astype(F32)
+            elif part == 0:
+                merged[:, at] = chips(at, y, yp, ym) + f_v[:, at].astype(F32)
+            else:
+                merged[:, at] += chips(at, y2)
             return carry
 
         lax.fori_loop(0, WIDTHS[j] // width, step, 0)
@@ -349,14 +382,17 @@
     def z_back():
         for yy in (yp, y2, ym):
             receive(y_s.at[yy], y_r.at[yy])
-        zf[piece(x, z)] = total(y_s, NY)
+        ours = piece(x, z)
+        zf[ours] = total(y_s, NY)
         for xx, zz in dp_peers:
-            send(zf.at[piece(x, z)], zf.at[piece(x, z)], 17, ag_r.at[dp], (xx * nz + zz, t))
+            send(zf.at[ours], zf.at[ours], 17, ag_r.at[dp], (xx * nz + zz, t))
+        send(zf.at[ours], zf.at[ours], 18, zf_r, sib)
 
     def z_cross():
         for xx, zz in dp_peers:
-            receive(zf.at[piece(xx, zz)], ag_r.at[xx * nz + zz])
-        send(zf.at[:, my_half], zf.at[:, my_half], 18, zf_r, sib)
+            theirs = piece(xx, zz)
+            receive(zf.at[theirs], ag_r.at[xx * nz + zz])
+            send(zf.at[theirs], zf.at[theirs], 18, zf_r, sib)
 
     def z_end():
         receive(zf.at[:, sib_half], zf_r)
@@ -365,14 +401,16 @@
         l1, l2, l3 = split3(linv_v[:, :RANK])
         lhs = jnp.concatenate([l1, l1, l2, l1, l2, l3], axis=1)
 
+        fw = d // 4
+
         def step(i, carry):
-            at = pl.ds(pl.multiple_of(i * zw, 128), zw)
+            at = pl.ds(pl.multiple_of(i * fw, 128), fw)
             z1, z2, z3 = split3(zf[:, at])
             rhs = jnp.concatenate([z1, z2, z1, z3, z2, z1], axis=0)
             right[:, at] = dot(lhs, rhs) * (1.0 / (nx * nz))
             return carry
 
-        lax.fori_loop(0, d // zw, step, 0)
+        lax.fori_loop(0, d // fw, step, 0)
 
     def leave():
         gather = [g_v.at[rows(t), :]] * 6 + [g_v.at[rows(t, 0, tok // 2), :]] * 2
@@ -386,7 +424,7 @@
             if sem in outgoing:
                 remote(ref, ref, send_sem.at[sem], own_r, sib).wait_send()
 
-    steps = dict(tell=tell, hear=hear, project_send=project_send, project_cross=project_cross,
+    steps = dict(tell=tell, hear=hear, hear_ring=hear_ring, project_send=project_send, project_cross=project_cross,
         enter=enter, wait_load=wait_load, absorb=absorb, own=own, direct=direct, relay=relay, cross=cross, opposite=opposite, pump=pump, merge=merge,
         project=project, carried=carried, flip=flip, left_start=left_start, left_second=left_second,
         left_end=left_end, mapped=mapped, mapped_send=mapped_send, mapped_relay=mapped_relay, z_first=z_first, mapped_end=mapped_end,
@@ -399,15 +437,19 @@
 
 def chain_plan():
     return [
-        ("enter",), ("tell", 0), ("direct", 0), ("project",), ("hear", 0), ("project_send",), ("direct", 1),
-        ("direct", 2), ("tell", 1), ("carried",), ("project_cross",), ("flip",), ("left_start",), ("own",),
-        ("pump", 0), ("pump", 1), ("hear", 1), ("tell", 2), ("left_second",), ("pump", 2), ("left_end",),
-        ("mapped",), ("mapped_send",), ("z_first",), ("pump", 3), ("mapped_relay",), ("pump", 4), ("hear", 2),
-        ("mapped_end",), ("z_send",), ("pump", 5), ("z_scatter",), ("factor",), ("pump", 6), ("merge", 0),
-        ("merge", 1), ("merge", 2), ("pump", 7), ("z_over_y",), ("merge", 3), ("merge", 4), ("merge", 5),
-        ("pump", 8), ("z_back",), ("pump", 9), ("merge", 6), ("merge", 7), ("pump", 10), ("z_cross",),
-        ("merge", 8), ("z_end",), ("pump", 11), ("finish",), ("merge", 9), ("pump", 12), ("merge", 10),
-        ("opposite", 11), ("merge", 11), ("opposite", 12), ("merge", 12), ("leave",),
+        ("enter",), ("direct", 0), ("project",), ("hear_ring",), ("project_send",), ("tell", 0), ("direct", 1),
+        ("direct", 2), ("direct", 3), ("direct", 4), ("hear", 0), ("tell", 1), ("carried",), ("hear", 1),
+        ("tell", 2), ("project_cross",), ("flip",), ("hear", 2), ("tell", 3), ("left_start",), ("own",),
+        ("pump", 0), ("hear", 3), ("tell", 4), ("pump", 1), ("left_second",), ("hear", 4), ("tell", 5),
+        ("pump", 2), ("pump", 3), ("pump", 4), ("left_end",), ("mapped",), ("mapped_send",), ("z_first",),
+        ("opposite", 0), ("mapped_relay",), ("pump", 5), ("opposite", 1), ("hear", 5), ("mapped_end",),
+        ("z_send",), ("pump", 6), ("opposite", 2), ("z_scatter",), ("factor",), ("pump", 7), ("opposite", 3),
+        ("merge", 0), ("merge", 1), ("merge", 2), ("pump", 8), ("opposite", 4), ("z_over_y",), ("pump", 9),
+        ("opposite", 5), ("merge", 3), ("merge", 4), ("z_back",), ("pump", 10), ("opposite", 6), ("merge", 5),
+        ("pump", 11), ("opposite", 7), ("merge", 6), ("merge", 7), ("merge", 8, 0), ("merge", 9, 0), ("pump", 12),
+        ("z_cross",), ("opposite", 8), ("opposite", 9), ("merge", 8, 1), ("opposite", 10), ("merge", 9, 1),
+        ("z_end",), ("finish",), ("merge", 10), ("opposite", 11), ("merge", 11, 0), ("merge", 12, 0),
+        ("opposite", 12), ("merge", 11, 1), ("merge", 12, 1), ("leave",),
     ]
 
 
@@ -495,7 +537,8 @@
             dma((nx * nz,)),
             dma,
             dma((22,)),
-            pltpu.SemaphoreType.REGULAR((3,)),
+            pltpu.SemaphoreType.REGULAR((6,)),
+            pltpu.SemaphoreType.REGULAR,
         ],
         compiler_params=pltpu.CompilerParams(
             collective_id=0, has_side_effects=True, vmem_limit_bytes=VMEM_LIMIT

time: 74.9 us -> 72.2 us (0.964)
  Pallas kernels: 73.9 us -> 71.2 us
    pallas_call x1, Pallas kernels: 69.6 us -> 66.9 us  [body(): pl.pallas_call(functools.partial(chain_kernel, nx, nz, chain_plan()), out...]
where the time goes in v3:
time: 72.2 us; the launch traced here: 72 us
  Pallas kernels  71.2 us (99%)
  between operations  0.8 us (1%)
    pallas_call x1, Pallas kernels, body(): pl.pallas_call(functools.partial(chain_kernel, nx, nz, chain_plan()), out...  66.9 us
    pallas_call x1, Pallas kernels, body(): pl.pallas_call(update_kernel, out_shape=(jax.ShapeDtypeStruct((feat, d),...  4.32 us

profile of v3, /device:TPU:1, one launch (start us, length us, event | category | flops | bytes accessed | tf_op | source)
XLA Modules:
  0.0 72.0 jit_solution(8761224893930447262)
XLA Ops:
  0.6 66.9 %gather_and_factors.1 = (f32[768,6144]{1,0:T(8,128)S(1)}, bf16[768,128]{1,0:T(8,128)(2,1)S(1)}, f32[32,6144]{1,0:T(8,128)S(1)}) custom-call(bf16[1024,768]{1,0:T(8,128)(2,1)} %a_hbm.1, bf16[128,6144]{1,0:T(8,128)(2,1)} %g_hbm.1, bf16[768,6144]{1,0:T(8,128)(2,1)} %bitcast.4, f32[32,6144]{1,0:T(8,128)} %bitcast.5), custom_call_target="tpu_custom_call" | custom-call | tf_op jit(solution)/shard_map/gather_and_factors/pallas_call | solution.py:487
  67.5 4.3 %update.1 = (bf16[768,6144]{1,0:T(8,128)(2,1)}, f32[32,6144]{1,0:T(8,128)}) custom-call(f32[768,6144]{1,0:T(8,128)S(1)} %get-tuple-element.7.merged, bf16[768,128]{1,0:T(8,128)(2,1)S(1)} %get-tuple-element.8.p3, f32[32,6144]{1,0:T(8,128)S(1)} %get-tuple-element.9.right), custom_call_target="tpu_custom_call" | custom-call | tf_op jit(solution)/shard_map/update/pallas_call | solution.py:550

commit v4 on v3

--- a/solution.py
+++ b/solution.py
@@ -12,10 +12,10 @@
 BF16 = jnp.bfloat16
 HIGHEST = lax.Precision.HIGHEST
 RANK = 32
-AHEAD = 5
+AHEAD = 4
 NY = 4
 NT = 8
-WIDTHS = (256,) + (512,) * 11 + (256,)
+WIDTHS = (512,) * 11 + (256, 256)
 STARTS = tuple(sum(WIDTHS[:k]) for k in range(len(WIDTHS)))
 CHUNKS = len(WIDTHS)
 ROWS_FIRST = (((1,), (0,)), ((), ()))
@@ -146,8 +146,6 @@
         loads[0].wait()
         loads[2].start()
         loads[3].start()
-        loads[1].wait()
-        q2_v[...] = jnp.concatenate(split2(q_v[...]), axis=0)
         pl.semaphore_wait(barrier, 3 + count(before))
         for device in ring:
             pl.semaphore_signal(ring_sem, 1, device_id=device, device_id_type=MESH)
@@ -239,6 +237,8 @@
     y_peers = (yp, y2, ym)
 
     def project():
+        loads[1].wait()
+        q2_v[...] = jnp.concatenate(split2(q_v[...]), axis=0)
         gq2 = dot(q2_v[...], g_v[rows(t), :], ROWS_BOTH)
         gq_s[c, y] = gq2[:RANK] + gq2[RANK:]
 
@@ -438,18 +438,17 @@
 def chain_plan():
     return [
         ("enter",), ("direct", 0), ("project",), ("hear_ring",), ("project_send",), ("tell", 0), ("direct", 1),
-        ("direct", 2), ("direct", 3), ("direct", 4), ("hear", 0), ("tell", 1), ("carried",), ("hear", 1),
-        ("tell", 2), ("project_cross",), ("flip",), ("hear", 2), ("tell", 3), ("left_start",), ("own",),
-        ("pump", 0), ("hear", 3), ("tell", 4), ("pump", 1), ("left_second",), ("hear", 4), ("tell", 5),
-        ("pump", 2), ("pump", 3), ("pump", 4), ("left_end",), ("mapped",), ("mapped_send",), ("z_first",),
-        ("opposite", 0), ("mapped_relay",), ("pump", 5), ("opposite", 1), ("hear", 5), ("mapped_end",),
-        ("z_send",), ("pump", 6), ("opposite", 2), ("z_scatter",), ("factor",), ("pump", 7), ("opposite", 3),
-        ("merge", 0), ("merge", 1), ("merge", 2), ("pump", 8), ("opposite", 4), ("z_over_y",), ("pump", 9),
-        ("opposite", 5), ("merge", 3), ("merge", 4), ("z_back",), ("pump", 10), ("opposite", 6), ("merge", 5),
-        ("pump", 11), ("opposite", 7), ("merge", 6), ("merge", 7), ("merge", 8, 0), ("merge", 9, 0), ("pump", 12),
-        ("z_cross",), ("opposite", 8), ("opposite", 9), ("merge", 8, 1), ("opposite", 10), ("merge", 9, 1),
-        ("z_end",), ("finish",), ("merge", 10), ("opposite", 11), ("merge", 11, 0), ("merge", 12, 0),
-        ("opposite", 12), ("merge", 11, 1), ("merge", 12, 1), ("leave",),
+        ("direct", 2), ("direct", 3), ("hear", 0), ("tell", 1), ("carried",), ("hear", 1), ("tell", 2),
+        ("project_cross",), ("flip",), ("hear", 2), ("tell", 3), ("left_start",), ("own",), ("pump", 0),
+        ("hear", 3), ("tell", 4), ("pump", 1), ("left_second",), ("hear", 4), ("tell", 5), ("pump", 2),
+        ("pump", 3), ("pump", 4), ("left_end",), ("mapped",), ("mapped_send",), ("z_first",), ("opposite", 0),
+        ("mapped_relay",), ("pump", 5), ("opposite", 1), ("hear", 5), ("mapped_end",), ("z_send",), ("pump", 6),
+        ("opposite", 2), ("z_scatter",), ("factor",), ("pump", 7), ("opposite", 3), ("merge", 0), ("merge", 1),
+        ("merge", 2), ("pump", 8), ("opposite", 4), ("z_over_y",), ("pump", 9), ("opposite", 5), ("merge", 3),
+        ("merge", 4), ("z_back",), ("pump", 10), ("opposite", 6), ("merge", 5), ("pump", 11), ("opposite", 7),
+        ("merge", 6), ("merge", 7), ("pump", 12), ("merge", 8, 0), ("merge", 9, 0), ("z_cross",), ("opposite", 8),
+        ("opposite", 9), ("opposite", 10), ("merge", 8, 1), ("merge", 9, 1), ("opposite", 11), ("merge", 10),
+        ("z_end",), ("opposite", 12), ("finish",), ("merge", 11), ("merge", 12), ("leave",),
     ]
 
 

time: 72.2 us -> 72.1 us (level)
  no operation moved by 1% of the time
where the time goes in v4:
time: 72.1 us; the launch traced here: 71.9 us
  Pallas kernels  71.1 us (99%)
  between operations  0.8 us (1%)
    pallas_call x1, Pallas kernels, body(): pl.pallas_call(functools.partial(chain_kernel, nx, nz, chain_plan()), out...  66.8 us
    pallas_call x1, Pallas kernels, body(): pl.pallas_call(update_kernel, out_shape=(jax.ShapeDtypeStruct((feat, d),...  4.32 us

profile of v4, /device:TPU:1, one launch (start us, length us, event | category | flops | bytes accessed | tf_op | source)
XLA Modules:
  0.0 71.9 jit_solution(7540284493068914209)
XLA Ops:
  0.6 66.8 %gather_and_factors.1 = (f32[768,6144]{1,0:T(8,128)S(1)}, bf16[768,128]{1,0:T(8,128)(2,1)S(1)}, f32[32,6144]{1,0:T(8,128)S(1)}) custom-call(bf16[1024,768]{1,0:T(8,128)(2,1)} %a_hbm.1, bf16[128,6144]{1,0:T(8,128)(2,1)} %g_hbm.1, bf16[768,6144]{1,0:T(8,128)(2,1)} %bitcast.4, f32[32,6144]{1,0:T(8,128)} %bitcast.5), custom_call_target="tpu_custom_call" | custom-call | tf_op jit(solution)/shard_map/gather_and_factors/pallas_call | solution.py:486
  67.4 4.3 %update.1 = (bf16[768,6144]{1,0:T(8,128)(2,1)}, f32[32,6144]{1,0:T(8,128)}) custom-call(f32[768,6144]{1,0:T(8,128)S(1)} %get-tuple-element.7.merged, bf16[768,128]{1,0:T(8,128)(2,1)S(1)} %get-tuple-element.8.p3, f32[32,6144]{1,0:T(8,128)S(1)} %get-tuple-element.9.right), custom_call_target="tpu_custom_call" | custom-call | tf_op jit(solution)/shard_map/update/pallas_call | solution.py:549

commit v5 on v4

--- a/solution.py
+++ b/solution.py
@@ -55,7 +55,7 @@
 def chain_kernel(
     nx, nz, plan,
     a_hbm, g_hbm, f_hbm, q_hbm,
-    merged, p3, right,
+    merged, p3, z_out, linv_out,
     a_v, at_v, g_v, f_v, q_v, q2_v, gq_s, fq_v,
     la1, lb1, la2, lb2, left_v, left2_v,
     al_send, al_sib, al_s, al_fwd, al_in, al2_v, linv_v,
@@ -398,19 +398,8 @@
         receive(zf.at[:, sib_half], zf_r)
 
     def finish():
-        l1, l2, l3 = split3(linv_v[:, :RANK])
-        lhs = jnp.concatenate([l1, l1, l2, l1, l2, l3], axis=1)
-
-        fw = d // 4
-
-        def step(i, carry):
-            at = pl.ds(pl.multiple_of(i * fw, 128), fw)
-            z1, z2, z3 = split3(zf[:, at])
-            rhs = jnp.concatenate([z1, z2, z1, z3, z2, z1], axis=0)
-            right[:, at] = dot(lhs, rhs) * (1.0 / (nx * nz))
-            return carry
-
-        lax.fori_loop(0, d // fw, step, 0)
+        z_out[...] = zf[...]
+        linv_out[...] = linv_v[...]
 
     def leave():
         gather = [g_v.at[rows(t), :]] * 6 + [g_v.at[rows(t, 0, tok // 2), :]] * 2
@@ -452,12 +441,12 @@
     ]
 
 
-def update_kernel(merged, p3, right, out, right_out, stage, r3_v, sems, right_sem):
+def update_kernel(replicas, merged, p3, z, linv, out, right_out, stage, r_v, r3_v, sems, right_sem):
     d = merged.shape[1]
     width = stage.shape[2]
     steps = d // width
-    right_copy = pltpu.make_async_copy(right, right_out, right_sem)
-    right_copy.start()
+    l1, l2, l3 = split3(linv[:, :RANK])
+    lhs = jnp.concatenate([l1, l1, l2, l1, l2, l3], axis=1)
 
     def block(i):
         return pl.ds(pl.multiple_of(i * width, 128), width)
@@ -466,13 +455,18 @@
         return pltpu.make_async_copy(stage.at[i], out.at[:, block(i)], sems.at[i])
 
     for i in range(steps):
-        r_high, r_low = split2(right[:, block(i)])
+        z1, z2, z3 = split3(z[:, block(i)])
+        rhs = jnp.concatenate([z1, z2, z1, z3, z2, z1], axis=0)
+        right = dot(lhs, rhs) * (1.0 / replicas)
+        r_v[:, block(i)] = right
+        r_high, r_low = split2(right)
         r3_v[...] = jnp.concatenate([r_high, r_low, r_high, jnp.zeros((RANK, width), BF16)], axis=0)
         stage[i] = (merged[:, block(i)] - dot(p3[...], r3_v[...])).astype(BF16)
         copy(i).start()
+        pltpu.make_async_copy(r_v.at[:, block(i)], right_out.at[:, block(i)], right_sem).start()
     for i in range(steps):
         copy(i).wait()
-    right_copy.wait()
+    pltpu.make_async_copy(r_v, right_out, right_sem).wait()
 
 
 def body(nx, nz, activations, out_grads, feedback, right_basis):
@@ -483,15 +477,16 @@
     any_spec = pl.BlockSpec(memory_space=pl.ANY)
     vmem_spec = pl.BlockSpec(memory_space=pltpu.VMEM)
     dma = pltpu.SemaphoreType.DMA
-    merged, p3, right = pl.pallas_call(
+    merged, p3, z, linv = pl.pallas_call(
         functools.partial(chain_kernel, nx, nz, chain_plan()),
         out_shape=(
             pltpu.VMEM((feat, d), F32),
             pltpu.VMEM((feat, 128), BF16),
             pltpu.VMEM((RANK, d), F32),
+            pltpu.VMEM((RANK, 128), F32),
         ),
         in_specs=[any_spec] * 4,
-        out_specs=(vmem_spec,) * 3,
+        out_specs=(vmem_spec,) * 4,
         scratch_shapes=[
             pltpu.VMEM((tokens, feat), BF16),
             pltpu.VMEM((feat, tokens), BF16),
@@ -547,22 +542,23 @@
     width = min(512, d // 2)
     vmem = functools.partial(pltpu.with_memory_space_constraint, memory_space=pltpu.VMEM)
     new_feedback, new_right = pl.pallas_call(
-        update_kernel,
+        functools.partial(update_kernel, nx * nz),
         out_shape=(
             jax.ShapeDtypeStruct((feat, d), BF16),
             jax.ShapeDtypeStruct((RANK, d), F32),
         ),
-        in_specs=[vmem_spec] * 3,
+        in_specs=[vmem_spec] * 4,
         out_specs=(any_spec, any_spec),
         scratch_shapes=[
             pltpu.VMEM((d // width, feat, width), BF16),
+            pltpu.VMEM((RANK, d), F32),
             pltpu.VMEM((128, width), BF16),
             dma((d // width,)),
             dma,
         ],
         compiler_params=pltpu.CompilerParams(vmem_limit_bytes=16 << 20),
         name="update",
-    )(vmem(merged), vmem(p3), vmem(right))
+    )(vmem(merged), vmem(p3), vmem(z), vmem(linv))
     return new_feedback[None], new_right.T
 
 

time: 72.1 us -> 72.3 us (level)
    pallas_call x1, Pallas kernels: 4.32 us -> 5.46 us  [body(): pl.pallas_call(functools.partial(update_kernel, nx * nz), out_shape=(jax....]
    pallas_call x1, Pallas kernels: 66.8 us -> 65.9 us  [body(): pl.pallas_call(functools.partial(chain_kernel, nx, nz, chain_plan()), out...]
where the time goes in v5:
time: 72.3 us; the launch traced here: 72.2 us
  Pallas kernels  71.4 us (99%)
  between operations  0.8 us (1%)
    pallas_call x1, Pallas kernels, body(): pl.pallas_call(functools.partial(chain_kernel, nx, nz, chain_plan()), out...  65.9 us
    pallas_call x1, Pallas kernels, body(): pl.pallas_call(functools.partial(update_kernel, nx * nz), out_shape=(jax....  5.46 us

profile of v5, /device:TPU:1, one launch (start us, length us, event | category | flops | bytes accessed | tf_op | source)
XLA Modules:
  0.0 72.2 jit_solution(17127838374757101223)
XLA Ops:
  0.6 65.9 %gather_and_factors.1 = (f32[768,6144]{1,0:T(8,128)S(1)}, bf16[768,128]{1,0:T(8,128)(2,1)S(1)}, f32[32,6144]{1,0:T(8,128)S(1)}, f32[32,128]{1,0:T(8,128)S(1)}) custom-call(bf16[1024,768]{1,0:T(8,128)(2,1)} %a_hbm.1, bf16[128,6144]{1,0:T(8,128)(2,1)} %g_hbm.1, bf16[768,6144]{1,0:T(8,128)(2,1)} %bitcast.4, f32[32,6144]{1,0:T(8,128)} %bitcast.5), custom_call_target="tpu_custom_call" | custom-call | tf_op jit(solution)/shard_map/gather_and_factors/pallas_call | solution.py:480
  66.5 5.5 %update.1 = (bf16[768,6144]{1,0:T(8,128)(2,1)}, f32[32,6144]{1,0:T(8,128)}) custom-call(f32[768,6144]{1,0:T(8,128)S(1)} %get-tuple-element.8.merged, bf16[768,128]{1,0:T(8,128)(2,1)S(1)} %get-tuple-element.9.p3, f32[32,6144]{1,0:T(8,128)S(1)} %get-tuple-element.10.z, f32[32,128]{1,0:T(8,128)S(1)} %get-tuple-element.11.linv), custom_call_target="tpu_custom_call" | custom-call | tf_op jit(solution)/shard_map/update/pallas_call | solution.py:544
